TPU v7x, 256 devices: a whole 4x4x8 slice. The times are simulated.
256 devices in a mesh: row: 64 (over z, x, core), col: 4 (over y).
Axes of the slice: x: 4, y: 4, z: 8, core: 2. Of those that a mesh axis runs over, the one named last changes fastest.
Arguments:
- new_embeddings: bfloat16 [32768, 1024], P('row'), may hold values from -6 to 6, as said below
- old_vectors: bfloat16 [16384, 1024], P(('col', 'row')), may hold values from -6 to 6, as said below
Outputs:
- gradient: float32 [32768, 1024], P('row', 'col')
- loss: float32 [], replicated
Inputs may be any that keep to these rules, and one draw needn't show every extreme that they name: `new_embeddings`: entries of order one. `old_vectors`: entries of order one.
All inputs are finite; a program needn't handle non-finite values.
Results may differ from a plain program's by a relative error of at most 0.0017.
Values may be sent and summed in bfloat16 or wider, within the bound.
A program may use at most 64 MiB of HBM per device.

v0:
```python
import math

import jax
import jax.numpy as jnp
from jax import lax
from jax.sharding import PartitionSpec as P

ITERS = 3


EPSILON = 0.01


def combined_all(value, axis, join):
    pieces = jax.tree.map(lambda part: lax.all_gather(part, axis), value)
    head = jax.tree.map(lambda part: part[0], pieces)
    tail = jax.tree.map(lambda part: part[1:], pieces)
    total, _ = lax.scan(lambda total, section: (join(total, section), None), head, tail)
    return total


def cost_block(block, old):
    row_norms = jnp.sum(jnp.square(block.astype(jnp.float32)), axis=1)
    old_norms = jnp.sum(jnp.square(old.astype(jnp.float32)), axis=1)
    inner = lax.dot_general(
        block, old, (((1,), (1,)), ((), ())), preferred_element_type=jnp.float32
    )
    return (row_norms[:, None] + old_norms[None, :] - 2.0 * inner) / block.shape[1]


def combine(first, second):
    top = jnp.maximum(first[0], second[0])
    return (top, first[1] * jnp.exp(first[0] - top) + second[1] * jnp.exp(second[0] - top))


def body(new_embeddings, old_vectors):
    rows = new_embeddings.shape[0]
    new_count = rows * lax.axis_size("row")
    gathered = lax.all_gather(old_vectors, "row", axis=0, tiled=True)
    cost_tile = cost_block(new_embeddings, gathered)
    old_count = cost_tile.shape[1] * lax.axis_size("col")
    col_pot = jnp.zeros((cost_tile.shape[1],), jnp.float32)
    for sweep in range(ITERS):
        scaled = (col_pot[None, :] - cost_tile) / EPSILON
        row_top = jnp.max(scaled, axis=1)
        row_sum = jnp.sum(jnp.exp(scaled - row_top[:, None]), axis=1)
        row_top, row_sum = combined_all((row_top, row_sum), "col", combine)
        row_pot = -EPSILON * math.log(old_count) - EPSILON * (row_top + jnp.log(row_sum))
        scaled = (row_pot[:, None] - cost_tile) / EPSILON
        col_top = jnp.max(scaled, axis=0)
        col_sum = jnp.sum(jnp.exp(scaled - col_top[None, :]), axis=0)
        col_top, col_sum = combined_all((col_top, col_sum), "row", combine)
        col_pot = -EPSILON * math.log(new_count) - EPSILON * (col_top + jnp.log(col_sum))
    plan = jnp.exp((row_pot[:, None] + col_pot[None, :] - cost_tile) / EPSILON)
    plan_low = plan.astype(jnp.bfloat16)
    loss_part = jnp.sum(plan * cost_tile)
    mass = jnp.sum(plan, axis=1)
    moved = jnp.dot(plan_low, gathered, preferred_element_type=jnp.float32)
    term = new_embeddings.astype(jnp.float32) * mass[:, None] - moved
    gradient = new_count * lax.psum_scatter(term, "col", scatter_dimension=1, tiled=True)
    loss = lax.psum(loss_part, ("row", "col"))
    return (gradient, loss)


def solution(mesh):
    placed = (P("row", None), P(("col", "row"), None))
    return jax.shard_map(
        body, mesh=mesh, in_specs=placed, out_specs=(P("row", "col"), P()), check_vma=False
    )
```

profile of v0, /device:TPU:1, one launch (start us, length us, event | category | flops | bytes accessed | tf_op | source)
XLA Modules:
  0.0 800.9 jit_solution(13700028531251998621)
XLA Ops:
  7.2 0.7 all-gather.26.cloned.1.call-update
  8.0 1.5 fusion.13
  9.5 88.5 %all-gather.26.cloned.1.call-done = bf16[4096,1024]{1,0:T(8,128)(2,1)} async-done(((bf16[64,1024]{1,0:T(8,128)(2,1)}), bf16[4096,1024]{1,0:T(8,128)(2,1)}) %all-gather.26.cloned.1.call-update) | async-done | bytes 8388624 | tf_op jit(solution)/shard_map/all_gather | solution.py:39
  98.0 5.2 multiply_reduce_fusion
  103.3 0.5 copy-done.1
  103.8 5.5 fusion.2
  109.3 3.2 copy-done
  112.5 2.0 exponential_reduce_fusion.5
  114.5 8.4 %all-gather.13 = f32[4,1,512]{2,1,0:T(1,128)S(1)} all-gather(f32[1,1,512]{2,1,0:T(1,128)S(1)} %bitcast.98), channel_id=3, replica_groups=mesh['row'=64,'col'=4] {'col'}, dimensions={0}, use_global_device_ids=true | all-gather | bytes 10240 | tf_op jit(solution)/shard_map/all_gather | solution.py:15
  122.9 8.1 %all-gather.12 = f32[4,1,512]{2,1,0:T(1,128)S(1)} all-gather(f32[1,1,512]{2,1,0:T(1,128)S(1)} %bitcast.95), channel_id=2, replica_groups=mesh['row'=64,'col'=4] {'col'}, dimensions={0}, use_global_device_ids=true | all-gather | bytes 10240 | tf_op jit(solution)/shard_map/all_gather | solution.py:15
  131.0 0.2 while.72
  131.2 4.6 fusion.3
  135.8 5.0 exponential_reduce_fusion.4
  140.9 0.7 all-gather.28.cloned.1.call-update
  141.5 0.2 all-gather.34.cloned.1.call-start
  141.8 77.1 %all-gather.30.cloned.1.call-done = f32[262144]{0:T(1024)} async-done(((f32[4096]{0:T(1024)}), f32[262144]{0:T(1024)}) %all-gather.30.cloned.1.call-update) | async-done | bytes 1048592 | tf_op jit(solution)/shard_map/all_gather | solution.py:15
  218.9 1.3 slice.139
  220.2 0.2 reshape.42
  220.4 76.0 %all-gather.28.cloned.1.call-done = f32[262144]{0:T(1024)} async-done(((f32[4096]{0:T(1024)}), f32[262144]{0:T(1024)}) %all-gather.28.cloned.1.call-update) | async-done | bytes 1048592 | tf_op jit(solution)/shard_map/all_gather | solution.py:15
  296.3 1.3 slice.138
  297.6 0.2 reshape.41
  297.8 0.7 slice.137
  298.5 0.7 slice.136
  299.2 5.0 while.73
  304.2 4.3 fusion.4
  308.6 4.5 exponential_reduce_fusion.3
  313.1 8.4 %all-gather.14 = f32[4,1,512]{2,1,0:T(1,128)S(1)} all-gather(f32[1,1,512]{2,1,0:T(1,128)S(1)} %bitcast.93), channel_id=6, replica_groups=mesh['row'=64,'col'=4] {'col'}, dimensions={0}, use_global_device_ids=true | all-gather | bytes 10240 | tf_op jit(solution)/shard_map/all_gather | solution.py:15
  321.5 8.1 %all-gather.15 = f32[4,1,512]{2,1,0:T(1,128)S(1)} all-gather(f32[1,1,512]{2,1,0:T(1,128)S(1)} %bitcast.96), channel_id=7, replica_groups=mesh['row'=64,'col'=4] {'col'}, dimensions={0}, use_global_device_ids=true | all-gather | bytes 10240 | tf_op jit(solution)/shard_map/all_gather | solution.py:15
  329.6 0.2 while.74
  329.7 4.6 fusion.5
  334.4 5.0 exponential_reduce_fusion.2
  339.4 0.0 all-gather.32.cloned.1.call-start
  339.4 0.5 all-gather.32.cloned.1.call-update
  340.0 77.9 %all-gather.34.cloned.1.call-done = f32[262144]{0:T(1024)} async-done(((f32[4096]{0:T(1024)}), f32[262144]{0:T(1024)}) %all-gather.34.cloned.1.call-update) | async-done | bytes 1048592 | tf_op jit(solution)/shard_map/all_gather | solution.py:15
  417.9 1.3 slice.147
  419.2 0.2 reshape.54
  419.4 75.8 %all-gather.32.cloned.1.call-done = f32[262144]{0:T(1024)} async-done(((f32[4096]{0:T(1024)}), f32[262144]{0:T(1024)}) %all-gather.32.cloned.1.call-update) | async-done | bytes 1048592 | tf_op jit(solution)/shard_map/all_gather | solution.py:15
  495.2 1.3 slice.146
  496.5 0.2 reshape.53
  496.7 0.7 slice.145
  497.4 0.7 slice.144
  498.1 5.0 while.75
  503.1 4.3 fusion.6
  507.5 4.5 exponential_reduce_fusion.1
  511.9 8.4 %all-gather.16 = f32[4,1,512]{2,1,0:T(1,128)S(1)} all-gather(f32[1,1,512]{2,1,0:T(1,128)S(1)} %bitcast.94), channel_id=10, replica_groups=mesh['row'=64,'col'=4] {'col'}, dimensions={0}, use_global_device_ids=true | all-gather | bytes 10240 | tf_op jit(solution)/shard_map/all_gather | solution.py:15
  520.3 8.1 %all-gather.17 = f32[4,1,512]{2,1,0:T(1,128)S(1)} all-gather(f32[1,1,512]{2,1,0:T(1,128)S(1)} %bitcast.97), channel_id=11, replica_groups=mesh['row'=64,'col'=4] {'col'}, dimensions={0}, use_global_device_ids=true | all-gather | bytes 10240 | tf_op jit(solution)/shard_map/all_gather | solution.py:15
  528.4 0.2 while.76
  528.6 5.2 fusion.7
  533.8 0.0 all-gather.38.cloned.1.call-start
  533.9 5.0 exponential_reduce_fusion
  538.9 0.3 reduce-scatter.2.cloned.1.call-start
  539.2 73.2 %all-gather.36.cloned.1.call-done = f32[262144]{0:T(1024)} async-done(((f32[4096]{0:T(1024)}), f32[262144]{0:T(1024)}) %all-gather.36.cloned.1.call-update) | async-done | bytes 1048592 | tf_op jit(solution)/shard_map/all_gather | solution.py:15
  612.4 1.3 slice.154
  613.7 0.2 reshape.65
  613.8 75.4 %all-gather.38.cloned.1.call-done = f32[262144]{0:T(1024)} async-done(((f32[4096]{0:T(1024)}), f32[262144]{0:T(1024)}) %all-gather.38.cloned.1.call-update) | async-done | bytes 1048592 | tf_op jit(solution)/shard_map/all_gather | solution.py:15
  689.2 1.3 slice.155
  690.5 0.2 reshape.66
  690.7 0.7 slice.152
  691.4 0.7 slice.153
  692.1 5.0 while.77
  697.2 7.0 multiply_reduce_fusion.1
  704.2 11.7 %fusion.14 = f32[512,1024]{1,0:T(8,128)} fusion(bf16[512,1024]{1,0:T(8,128)(2,1)S(1)} %copy-done.3, bf16[4096,1024]{1,0:T(8,128)(2,1)} %all-gather.26.cloned.1.call-done, f32[512,4096]{1,0:T(8,128)} %copy-done, f32[4096]{0:T(1024)S(1)} %multiply_subtract_fusion, f32[512]{0:T(512)S(1)} %multiply_subtract_fusion.3, f32[512]{0:T(512)S(1)} %get-tuple-element.183), kind=kOutput, calls=%fused_computation.49 | convolution fusion | flops 4304928768 | bytes 19943424 | tf_op jit(solution)/shard_map/dot_general | solution.py:58
  715.9 76.3 %psum.7 = f32[]{:T(128)} all-reduce(f32[]{:T(128)} %get-tuple-element.182), channel_id=1, replica_groups=mesh['row'=64,'col'=4] {'row','col'}, use_global_device_ids=true, to_apply=%region_29.30 | all-reduce | flops 1 | bytes 8 | tf_op jit(solution)/shard_map/psum | solution.py:61
  792.2 1.9 broadcast_multiply_fusion
  (440 shorter events, 10.8 us)
Async XLA Ops:
  7.2 96.1 %copy-start.2 = (bf16[512,1024]{1,0:T(8,128)(2,1)S(1)}, bf16[512,1024]{1,0:T(8,128)(2,1)}, u32[]{:S(2)}) copy-start(bf16[512,1024]{1,0:T(8,128)(2,1)} %param.14) | copy-start | bytes 3145732
  7.2 90.8 %all-gather.26.cloned.1.call-start = ((), (), s32[]{:S(2)}) async-start(), calls=%async_computation.1 | async-start | bytes 8519680 | tf_op jit(solution)/shard_map/all_gather | solution.py:39
  7.9 211.0 %all-gather.30.cloned.1.call-start = ((), (), s32[]{:S(2)}) async-start(), calls=%async_computation.4 | async-start | bytes 1064960 | tf_op jit(solution)/shard_map/all_gather | solution.py:15
  98.0 5.8 copy-start.1
  109.3 3.2 copy-start
  135.8 5.1 copy-start.4
  140.8 155.5 %all-gather.28.cloned.1.call-start = ((), (), s32[]{:S(2)}) async-start(), calls=%async_computation.3 | async-start | bytes 1064960 | tf_op jit(solution)/shard_map/all_gather | solution.py:15
  141.5 276.4 %all-gather.34.cloned.1.call-start = ((), (), s32[]{:S(2)}) async-start(), calls=%async_computation.6 | async-start | bytes 1064960 | tf_op jit(solution)/shard_map/all_gather | solution.py:15
  334.3 5.1 copy-start.5
  339.4 155.8 %all-gather.32.cloned.1.call-start = ((), (), s32[]{:S(2)}) async-start(), calls=%async_computation.5 | async-start | bytes 1064960 | tf_op jit(solution)/shard_map/all_gather | solution.py:15
  340.0 272.4 %all-gather.36.cloned.1.call-start = ((), (), s32[]{:S(2)}) async-start(), calls=%async_computation.7 | async-start | bytes 1064960 | tf_op jit(solution)/shard_map/all_gather | solution.py:15
  533.8 155.4 %all-gather.38.cloned.1.call-start = ((), (), s32[]{:S(2)}) async-start(), calls=%async_computation.8 | async-start | bytes 1064960 | tf_op jit(solution)/shard_map/all_gather | solution.py:15
  538.9 253.3 %reduce-scatter.2.cloned.1.call-start = ((), (), s32[]{:S(2)}) async-start(), calls=%async_computation.2 | async-start | bytes 2621440 | tf_op jit(solution)/shard_map/reduce_scatter | solution.py:60
  697.1 7.1 copy-start.3
Sparse Core Ops, SparseCore 0:
  10.8 87.1 all-gather.25
  140.9 77.9 all-gather.29
  222.2 74.0 all-gather.27
  339.5 78.3 all-gather.33
  421.1 74.0 all-gather.31
  534.0 78.3 all-gather.35
  615.1 74.0 all-gather.37
  716.0 30.3 reduce-scatter.1
where the time goes:
time: 802 us; the launch traced here: 801 us
  waiting for transfers between devices  546 us (68%)
  blocking collectives  126 us (16%)
  other arithmetic  69.2 us (9%)
  local copies, waits for them, and re-layouts  22.8 us (3%)
  matrix products  17.2 us (2%)
  between operations  14.4 us (2%)
    all_gather x6, waiting for transfers between devices, combined_all(): pieces = jax.tree.map(lambda part: lax.all_gather(part, axis), value)  455 us
    all_gather x1, waiting for transfers between devices, body(): gathered = lax.all_gather(old_vectors, 'row', axis=0, tiled=True)  88.5 us
    psum x1, blocking collectives, body(): loss = lax.psum(loss_part, ('row', 'col'))  76.3 us
    all_gather x6, blocking collectives, combined_all(): pieces = jax.tree.map(lambda part: lax.all_gather(part, axis), value)  49.5 us
  transfers between devices with their start and end apart: 8, of which 7 were waited for; matrix products, arithmetic and copies ran while one was open for 1% of the time, Pallas kernels for 0%

commit v1 on v0

v1 whole, which is shorter than its diff:
```python
import math

import jax
import jax.numpy as jnp
from jax import lax
from jax.experimental import pallas as pl
from jax.experimental.pallas import tpu as pltpu
from jax.sharding import PartitionSpec as P

MESH = pl.DeviceIdType.MESH
EPSILON = 0.01
RATE = math.log2(math.e) / EPSILON
LIFT = 40.0

NX, NCORE, NY = 4, 2, 4
SUB = 32


def body_kernel(
    x_hbm, y_hbm, g_ref, loss_ref,
    xc, yg, cost, ex, plan_low, xn, top, tot, rowb, yn, vcol, tcol,
    rs1, rr1, rs2, rr2,
    cxs1, cxr1, czs1, czr1, cxs2, cxr2, czs2, czr2,
    lzs, lzr, lxs, lxr, lys, lyr,
    half_out, half_own, half_in, part_out, part_in,
    local_sem, xcore_sem, gsend, ax_sem, az_sem, bz_sem, bx_sem,
    ex_send, ex_recv, hs_sem, hr_sem, ps_sem, pr_sem,
):
    rows, depth = x_hbm.shape
    shard = y_hbm.shape[0]
    nrow, ncol = cost.shape
    nz = lax.axis_size("row") // (NX * NCORE)
    r = lax.axis_index("row")
    y = lax.axis_index("col")
    z = r // (NX * NCORE)
    x = (r // NCORE) % NX
    c = r % NCORE
    new_total = rows * lax.axis_size("row")
    old_total = shard * lax.axis_size("row") * lax.axis_size("col")
    lanes_a = 3 * depth // 8
    reach = nz // 2

    def dev(dz=0, dx=0, dc=0, dy=0):
        zz = lax.rem(z + dz + nz, nz)
        xx = lax.rem(x + dx + NX, NX)
        cc = lax.rem(c + dc, NCORE)
        yy = lax.rem(y + dy + NY, NY)
        return ((zz * NX + xx) * NCORE + cc, yy)

    z_peers = [dev(dz=d) for d in range(1, nz)]
    x_peers = [dev(dx=d) for d in range(1, NX)]
    y_peers = [dev(dy=d, dc=e) for d in range(NY) for e in range(NCORE) if d or e]

    barrier = pltpu.get_barrier_semaphore()
    everyone = z_peers + x_peers + y_peers
    for p in everyone:
        pl.semaphore_signal(barrier, inc=1, device_id=p, device_id_type=MESH)
    pl.semaphore_wait(barrier, len(everyone))

    part_lanes = {"a": pl.ds(0, lanes_a), "b": pl.ds(lanes_a, depth - lanes_a)}

    def region(dz, dx, part, half=None):
        slot = lax.rem(z + dz + nz, nz) * NX + lax.rem(x + dx + NX, NX)
        first = 0 if half is None else half * (shard // 2)
        count = shard if half is None else shard // 2
        start = pl.multiple_of(slot * shard + first, shard // 2)
        return yg.at[pl.ds(start, count), part_lanes[part]]

    def send(part, dst, sem, target, half=None, own=False):
        src = dst
        if own:
            src = y_hbm.at[:, part_lanes[part]]
        pltpu.make_async_remote_copy(
            src, dst, gsend.at[0 if part == "a" else 1], sem, device_id=target, device_id_type=MESH
        ).start()

    def arrived(ref, sem):
        pltpu.make_async_copy(ref, ref, sem).wait()

    zstep = (dev(dz=1), dev(dz=-1))
    xstep = (dev(dx=1), dev(dx=-1))
    xi_of = (0, -1, 1, 2)
    order_dz = [0] + [s * d for d in range(1, reach) for s in (-1, 1)] + [reach]
    place = {dz: i for i, dz in enumerate(order_dz)}

    def send_bx(dz, own=False):
        for way in (0, 1):
            send("b", region(dz, 0, "b"), bx_sem.at[place[dz], way], xstep[way], own=own)

    def send_az(xi, own=False):
        for way in (0, 1):
            send("a", region(0, xi_of[xi], "a"), az_sem.at[way, 0, xi], zstep[way], own=own)

    def on_ax(k):
        if k < 2:
            dx = -1 if k == 0 else 1
            arrived(region(0, dx, "a"), ax_sem.at[k])
            send("a", region(0, dx, "a", k), ax_sem.at[2 + k], xstep[k])
            send_az(1 + k)
        else:
            arrived(region(0, -2 if k == 2 else 2, "a", k - 2), ax_sem.at[k])
            if k == 3:
                send_az(3)

    def on_ring(part, way, d, dx, sems):
        sign = -1 if way == 0 else 1
        if d < reach:
            arrived(region(sign * d, dx, part), sems(d - 1))
            if d < reach - 1:
                send(part, region(sign * d, dx, part), sems(d), zstep[way])
            else:
                send(part, region(sign * d, dx, part, way), sems(d), zstep[way])
        else:
            arrived(region(sign * d, dx, part, way), sems(d - 1))

    def on_az(d, xi):
        for way in (0, 1):
            on_ring("a", way, d, xi_of[xi], lambda i: az_sem.at[way, i, xi])

    def on_bz(d):
        for way in (0, 1):
            on_ring("b", way, d, 0, lambda i: bz_sem.at[way, i])
            if d < reach:
                send_bx(-d if way == 0 else d)
        if d == reach:
            send_bx(reach)

    def on_bx(dz, k):
        i = place[dz]
        if k < 2:
            dx = -1 if k == 0 else 1
            arrived(region(dz, dx, "b"), bx_sem.at[i, k])
            send("b", region(dz, dx, "b", k), bx_sem.at[i, 2 + k], xstep[k])
        else:
            arrived(region(dz, -2 if k == 2 else 2, "b", k - 2), bx_sem.at[i, k])

    own_slot = pl.ds(pl.multiple_of((z * NX + x) * shard, shard), shard)
    own_rows = pl.ds(pl.multiple_of(c * rows, rows), rows)
    other_rows = pl.ds(pl.multiple_of((1 - c) * rows, rows), rows)

    for way in (0, 1):
        send("b", region(0, 0, "b"), bz_sem.at[way, 0], zstep[way], own=True)
        send("a", region(0, 0, "a"), ax_sem.at[way], xstep[way], own=True)
    send_az(0, own=True)
    send_bx(0, own=True)
    x_copy = pltpu.make_async_remote_copy(
        x_hbm, xc.at[own_rows], xcore_sem.at[0], xcore_sem.at[1], device_id=dev(dc=1), device_id_type=MESH
    )
    x_copy.start()
    x_local = pltpu.make_async_copy(x_hbm, xc.at[own_rows], local_sem.at[0])
    y_local = pltpu.make_async_copy(y_hbm, yg.at[own_slot], local_sem.at[1])
    x_local.start()
    y_local.start()

    top[...] = jnp.full(top.shape, 1e30, jnp.float32)
    tot[...] = jnp.zeros(tot.shape, jnp.float32)

    def row_norms(half):
        def step(i, carry):
            rs = pl.ds(pl.multiple_of(half * rows + i * SUB, SUB), SUB)
            v = jnp.square(xc[rs, :].astype(jnp.float32))
            xn[rs, :] = jnp.broadcast_to(jnp.sum(v, axis=1, keepdims=True), (SUB, 128))
            return carry

        lax.fori_loop(0, rows // SUB, step, 0)

    group = NX * shard
    tile = 256

    def compute(dz):
        col0 = pl.multiple_of(lax.rem(z + dz + nz, nz) * group, group)
        cols = pl.ds(col0, group)
        sq = jnp.square(yg[cols, :].astype(jnp.float32))
        high = sq.astype(jnp.bfloat16)
        low = (sq - high.astype(jnp.float32)).astype(jnp.bfloat16)
        ones = jnp.ones((16, depth), jnp.bfloat16)
        nt = (((1,), (1,)), ((), ()))
        norms = lax.dot_general(ones, high, nt, preferred_element_type=jnp.float32)
        norms = norms + lax.dot_general(ones, low, nt, preferred_element_type=jnp.float32)
        yn[:, cols] = norms[0:1, :]

        def step(i, carry):
            r0 = pl.multiple_of(i * tile, tile)
            rs = pl.ds(r0, tile)
            inner = lax.dot_general(xc[rs, :], yg[cols, :], nt, preferred_element_type=jnp.float32)
            best = top[rs, :]
            parts = []
            xrow = xn[rs, :]
            for b in range(group // 128):
                cs = pl.ds(pl.multiple_of(col0 + b * 128, 128), 128)
                val = (xrow + yn[:, cs] - 2.0 * inner[:, b * 128 : (b + 1) * 128]) * (1.0 / depth)
                cost[rs, cs] = val
                parts.append(val)
            low_ = best
            for val in parts:
                low_ = jnp.minimum(low_, val)
            acc = tot[rs, :] * jnp.exp2((low_ - best) * RATE)
            for val in parts:
                acc = acc + jnp.exp2((low_ - val) * RATE)
            top[rs, :] = low_
            tot[rs, :] = acc
            return carry

        lax.fori_loop(0, nrow // tile, step, 0)

    on_ax(0)
    on_ax(1)
    on_bz(1)
    on_az(1, 0)
    on_bx(0, 0)
    on_bx(0, 1)
    on_ax(2)
    on_ax(3)
    on_az(1, 1)
    on_az(1, 2)
    x_local.wait()
    y_local.wait()
    x_copy.wait()
    row_norms(0)
    row_norms(1)
    on_bx(0, 2)
    on_bx(0, 3)
    on_az(1, 3)
    on_bz(2)
    compute(0)
    for k in (0, 1):
        on_bx(-1, k)
        on_bx(1, k)
    for xi in range(4):
        on_az(2, xi)
    for k in (2, 3):
        on_bx(-1, k)
        on_bx(1, k)
    on_bz(3)
    compute(-1)
    for k in (0, 1):
        on_bx(-2, k)
        on_bx(2, k)
    compute(1)
    for xi in range(4):
        on_az(3, xi)
    on_bz(4)
    for k in (2, 3):
        on_bx(-2, k)
        on_bx(2, k)
    for k in (0, 1):
        on_bx(-3, k)
        on_bx(3, k)
    compute(-2)
    for k in (0, 1):
        on_bx(4, k)
    compute(2)
    for k in (2, 3):
        on_bx(-3, k)
        on_bx(3, k)
    compute(-3)
    compute(3)
    for xi in range(4):
        on_az(4, xi)
    for k in (2, 3):
        on_bx(4, k)
    compute(4)

    def start(send_ref, recv_ref, i, peers):
        for j, p in enumerate(peers):
            pltpu.make_async_remote_copy(
                send_ref, recv_ref.at[j], ex_send.at[i], ex_recv.at[i], device_id=p, device_id_type=MESH
            ).start()

    def finish(recv_ref, i):
        pltpu.make_async_copy(recv_ref, recv_ref, ex_recv.at[i]).wait()
        pltpu.make_async_copy(recv_ref, recv_ref, ex_send.at[i]).wait()

    def to_rows(line):
        return jnp.transpose(jnp.broadcast_to(line, (128, nrow)))

    top_t = jnp.transpose(top[...])
    tot_t = jnp.transpose(tot[...])
    low = jnp.min(top_t, axis=0, keepdims=True)
    mass = jnp.sum(tot_t * jnp.exp2((low - top_t) * RATE), axis=0, keepdims=True)
    rs1[:, 0:nrow] = low
    rs1[:, nrow : 2 * nrow] = mass
    start(rs1, rr1, 0, y_peers)
    finish(rr1, 0)
    lows = [low] + [rr1[j, :, 0:nrow] for j in range(len(y_peers))]
    masses = [mass] + [rr1[j, :, nrow : 2 * nrow] for j in range(len(y_peers))]
    low = lows[0]
    for v in lows[1:]:
        low = jnp.minimum(low, v)
    mass = sum(m * jnp.exp2((low - v) * RATE) for v, m in zip(lows, masses))
    rowb[...] = to_rows(low * RATE - jnp.log2(mass) - math.log2(old_total))

    nb = ncol // 128

    def fold(v, join):
        out = v[0:8]
        for i in range(1, v.shape[0] // 8):
            out = join(out, v[8 * i : 8 * i + 8])
        return out

    def highest(i, carry):
        rs = pl.ds(pl.multiple_of(i * SUB, SUB), SUB)
        rb = rowb[rs, :]
        out = []
        for b in range(nb):
            cs = pl.ds(b * 128, 128)
            a = rb - cost[rs, cs] * RATE
            ex[rs, cs] = a
            out.append(jnp.maximum(carry[b], fold(a, jnp.maximum)))
        return tuple(out)

    carry = lax.fori_loop(
        0, nrow // SUB, highest, tuple(jnp.full((8, 128), -3e38, jnp.float32) for _ in range(nb))
    )
    for b in range(nb):
        tcol[:, b * 128 : (b + 1) * 128] = jnp.max(carry[b], axis=0, keepdims=True)

    def scaled(i, carry):
        rs = pl.ds(pl.multiple_of(i * SUB, SUB), SUB)
        out = []
        for b in range(nb):
            cs = pl.ds(b * 128, 128)
            e = jnp.exp2(ex[rs, cs] - (tcol[:, cs] - LIFT))
            ex[rs, cs] = e
            out.append(carry[b] + fold(e, jnp.add))
        return tuple(out)

    zeros = tuple(jnp.zeros((8, 128), jnp.float32) for _ in range(nb))
    carry = lax.fori_loop(0, nrow // SUB, scaled, zeros)
    cxs1[:, 0:ncol] = tcol[...]
    for b in range(nb):
        cxs1[:, ncol + b * 128 : ncol + (b + 1) * 128] = jnp.sum(carry[b], axis=0, keepdims=True)

    def merge(own, recv, n):
        tops = [own[:, 0:ncol]] + [recv[j, :, 0:ncol] for j in range(n)]
        sums = [own[:, ncol:]] + [recv[j, :, ncol:] for j in range(n)]
        best = tops[0]
        for v in tops[1:]:
            best = jnp.maximum(best, v)
        return best, sum(s * jnp.exp2(v - best) for v, s in zip(tops, sums))

    start(cxs1, cxr1, 1, x_peers)
    finish(cxr1, 1)
    best, total = merge(cxs1[...], cxr1, len(x_peers))
    czs1[:, 0:ncol] = best
    czs1[:, ncol:] = total
    start(czs1, czr1, 2, z_peers)
    finish(czr1, 2)
    best, total = merge(czs1[...], czr1, len(z_peers))
    grow = 2.0 ** (2 * LIFT) / new_total
    vcol[...] = jnp.exp2(tcol[...] - best) * grow / total

    for sweep in range(2):
        def row_sums(i, carry):
            rs = pl.ds(pl.multiple_of(i * SUB, SUB), SUB)
            acc = ex[rs, 0:128] * vcol[:, 0:128]
            for b in range(1, nb):
                cs = pl.ds(b * 128, 128)
                acc = acc + ex[rs, cs] * vcol[:, cs]
            tot[rs, :] = acc
            return carry

        lax.fori_loop(0, nrow // SUB, row_sums, 0)
        line = jnp.sum(jnp.transpose(tot[...]), axis=0, keepdims=True)
        i = 3 + 3 * sweep
        rs2[sweep] = line
        start(rs2.at[sweep], rr2.at[sweep], i, y_peers)
        finish(rr2.at[sweep], i)
        line = line + sum(rr2[sweep, j] for j in range(len(y_peers)))
        rowb[...] = to_rows((2.0 ** (2 * LIFT) / old_total) / line)

        def col_sums(i, carry):
            rs = pl.ds(pl.multiple_of(i * SUB, SUB), SUB)
            rb = rowb[rs, :]
            return tuple(
                carry[b] + fold(ex[rs, pl.ds(b * 128, 128)] * rb, jnp.add) for b in range(nb)
            )

        carry = lax.fori_loop(0, nrow // SUB, col_sums, zeros)
        for b in range(nb):
            cs = pl.ds(b * 128, 128)
            cxs2[sweep, :, cs] = vcol[:, cs] * jnp.sum(carry[b], axis=0, keepdims=True)
        start(cxs2.at[sweep], cxr2.at[sweep], i + 1, x_peers)
        finish(cxr2.at[sweep], i + 1)
        czs2[sweep] = cxs2[sweep] + sum(cxr2[sweep, j] for j in range(len(x_peers)))
        start(czs2.at[sweep], czr2.at[sweep], i + 2, z_peers)
        finish(czr2.at[sweep], i + 2)
        total = czs2[sweep] + sum(czr2[sweep, j] for j in range(len(z_peers)))
        vcol[...] = vcol[...] * (grow / total)

    def planned(i, carry):
        rs = pl.ds(pl.multiple_of(i * SUB, SUB), SUB)
        rb = rowb[rs, :] * 2.0 ** (-2 * LIFT)
        mass = jnp.zeros((SUB, 128), jnp.float32)
        part = jnp.zeros((SUB, 128), jnp.float32)
        for b in range(nb):
            cs = pl.ds(b * 128, 128)
            p = ex[rs, cs] * rb * vcol[:, cs]
            plan_low[rs, cs] = p.astype(jnp.bfloat16)
            mass = mass + p
            part = part + p * cost[rs, cs]
        tot[rs, :] = jnp.broadcast_to(jnp.sum(mass, axis=1, keepdims=True), (SUB, 128))
        return carry + fold(part, jnp.add)

    part = lax.fori_loop(0, nrow // SUB, planned, jnp.zeros((8, 128), jnp.float32))
    lzs[...] = jnp.sum(part, axis=0, keepdims=True)
    start(lzs, lzr, 9, z_peers)

    width = g_ref.shape[1]
    turn = (2, 1, 3, 0)
    y_target = {d: dev(dy=d) for d in (1, 2, 3)}

    def product(ci):
        q = lax.rem(y + turn[ci], NY)
        lanes = pl.ds(pl.multiple_of(q * width, width), width)
        for which, out in ((other_rows, half_out), (own_rows, half_own)):
            base = (1 - c) * rows if out is half_out else c * rows

            def step(i, carry):
                rs = pl.ds(pl.multiple_of(base + i * tile, tile), tile)
                moved = jnp.dot(plan_low[rs, :], yg[:, lanes], preferred_element_type=jnp.float32)
                m = tot[rs, :]
                xs = xc[rs, lanes].astype(jnp.float32)
                os = pl.ds(pl.multiple_of(i * tile, tile), tile)
                for b in range(width // 128):
                    cs = slice(b * 128, (b + 1) * 128)
                    out[ci, os, cs] = xs[:, cs] * m - moved[:, cs]
                return carry

            lax.fori_loop(0, rows // tile, step, 0)
            if out is half_out:
                half_copy(ci).start()

    def half_copy(ci):
        return pltpu.make_async_remote_copy(
            half_out.at[ci], half_in.at[ci], hs_sem.at[ci], hr_sem.at[ci],
            device_id=dev(dc=1), device_id_type=MESH,
        )

    def part_copy(ci):
        return pltpu.make_async_remote_copy(
            part_out.at[ci], part_in.at[ci], ps_sem.at[ci], pr_sem.at[ci],
            device_id=y_target[turn[ci]], device_id_type=MESH,
        )

    def pass_on(ci):
        half_copy(ci).wait()
        part_out[ci] = (half_own[ci] + half_in[ci]).astype(jnp.bfloat16)
        part_copy(ci).start()

    product(0)
    product(1)
    pass_on(0)
    finish(lzr, 9)
    lxs[...] = lzs[...] + sum(lzr[j] for j in range(len(z_peers)))
    start(lxs, lxr, 10, x_peers)
    product(2)
    pass_on(1)
    product(3)
    pass_on(2)
    finish(lxr, 10)
    lys[...] = lxs[...] + sum(lxr[j] for j in range(len(x_peers)))
    start(lys, lyr, 11, y_peers)
    half_copy(3).wait()
    half_own[3] = half_own[3] + half_in[3]
    finish(lyr, 11)
    loss = lys[...] + sum(lyr[j] for j in range(len(y_peers)))
    loss_ref[...] = jnp.broadcast_to(jnp.sum(loss, axis=1, keepdims=True), loss_ref.shape)
    for ci in (0, 1, 2):
        part_copy(ci).wait()
    g_ref[...] = float(new_total) * (
        half_own[3] + part_in[0].astype(jnp.float32) + part_in[1].astype(jnp.float32) + part_in[2].astype(jnp.float32)
    )
    others = (nz * NX - 1) * shard
    for i, part in ((0, "a"), (1, "b")):
        sent = yg.at[pl.ds(0, others), part_lanes[part]]
        pltpu.make_async_copy(sent, sent, gsend.at[i]).wait()


def solution(mesh):
    def body(new_embeddings, old_vectors):
        rows, depth = new_embeddings.shape
        shard = old_vectors.shape[0]
        nz = lax.axis_size("row") // (NX * NCORE)
        nrow, ncol = rows * NCORE, shard * nz * NX
        width = depth // NY
        f32, bf16 = jnp.float32, jnp.bfloat16
        ny, npx, npz = NY * NCORE - 1, NX - 1, nz - 1
        dma = pltpu.SemaphoreType.DMA
        scratch = [
            pltpu.VMEM((nrow, depth), bf16),
            pltpu.VMEM((ncol, depth), bf16),
            pltpu.VMEM((nrow, ncol), f32),
            pltpu.VMEM((nrow, ncol), f32),
            pltpu.VMEM((nrow, ncol), bf16),
            pltpu.VMEM((nrow, 128), f32),
            pltpu.VMEM((nrow, 128), f32),
            pltpu.VMEM((nrow, 128), f32),
            pltpu.VMEM((nrow, 128), f32),
            pltpu.VMEM((1, ncol), f32),
            pltpu.VMEM((1, ncol), f32),
            pltpu.VMEM((1, ncol), f32),
            pltpu.VMEM((1, 2 * nrow), f32),
            pltpu.VMEM((ny, 1, 2 * nrow), f32),
            pltpu.VMEM((2, 1, nrow), f32),
            pltpu.VMEM((2, ny, 1, nrow), f32),
            pltpu.VMEM((1, 2 * ncol), f32),
            pltpu.VMEM((npx, 1, 2 * ncol), f32),
            pltpu.VMEM((1, 2 * ncol), f32),
            pltpu.VMEM((npz, 1, 2 * ncol), f32),
            pltpu.VMEM((2, 1, ncol), f32),
            pltpu.VMEM((2, npx, 1, ncol), f32),
            pltpu.VMEM((2, 1, ncol), f32),
            pltpu.VMEM((2, npz, 1, ncol), f32),
            pltpu.VMEM((1, 128), f32),
            pltpu.VMEM((npz, 1, 128), f32),
            pltpu.VMEM((1, 128), f32),
            pltpu.VMEM((npx, 1, 128), f32),
            pltpu.VMEM((1, 128), f32),
            pltpu.VMEM((ny, 1, 128), f32),
            pltpu.VMEM((4, rows, width), f32),
            pltpu.VMEM((4, rows, width), f32),
            pltpu.VMEM((4, rows, width), f32),
            pltpu.VMEM((3, rows, width), bf16),
            pltpu.VMEM((3, rows, width), bf16),
            dma((2,)),
            dma((2,)),
            dma((2,)),
            dma((4,)),
            dma((2, nz // 2, 4)),
            dma((2, nz // 2)),
            dma((nz, 4)),
            dma((12,)),
            dma((12,)),
            dma((4,)),
            dma((4,)),
            dma((3,)),
            dma((3,)),
        ]
        gradient, loss = pl.pallas_call(
            body_kernel,
            out_shape=(
                jax.ShapeDtypeStruct((rows, width), f32),
                jax.ShapeDtypeStruct((1, 128), f32),
            ),
            in_specs=[pl.BlockSpec(memory_space=pl.ANY)] * 2,
            out_specs=[pl.BlockSpec(memory_space=pltpu.VMEM)] * 2,
            scratch_shapes=scratch,
            compiler_params=pltpu.CompilerParams(
                collective_id=0, has_side_effects=True, vmem_limit_bytes=56 << 20
            ),
            name="sinkhorn",
        )(new_embeddings, old_vectors)
        return gradient, loss[0, 0]

    placed = (P("row", None), P(("col", "row"), None))
    return jax.shard_map(
        body, mesh=mesh, in_specs=placed, out_specs=(P("row", "col"), P()), check_vma=False
    )
```

time: 802 us -> 120 us (0.15)
  waiting for transfers between devices: 546 us -> 0 us
  blocking collectives: 126 us -> 0 us
  Pallas kernels: 0 us -> 116 us
  other arithmetic: 69.2 us -> 0 us
  local copies, waits for them, and re-layouts: 22.8 us -> 1.87 us
  matrix products: 17.2 us -> 0 us
  between operations: 14.4 us -> 1.81 us
    all_gather x7 -> x0, waiting for transfers between devices: 544 us -> none  [the longest x6 455 us: combined_all(): pieces = jax.tree.map(lambda part: lax.all_gather(part, axis), value)]
    pallas_call x0 -> x1, Pallas kernels: none -> 116 us  [body(): pl.pallas_call(body_kernel, out_shape=(jax.ShapeDtypeStruct((rows, width)...]
    psum x1 -> x0, blocking collectives: 76.3 us -> none  [body(): loss = lax.psum(loss_part, ('row', 'col'))]
    all_gather x6 -> x0, blocking collectives: 49.5 us -> none  [combined_all(): pieces = jax.tree.map(lambda part: lax.all_gather(part, axis), value)]
    reduce_sum x9 -> x0, other arithmetic: 39.7 us -> none  [the longest x3 15 us: body(): col_sum = jnp.sum(jnp.exp(scaled - col_top[None, :]), axis=0)]
    reduce_max x5 -> x0, other arithmetic: 23.1 us -> none  [the longest x3 14.4 us: body(): col_top = jnp.max(scaled, axis=0)]
    dot_general x2 -> x0, matrix products: 17.2 us -> none  [the longest x1 11.7 us: body(): moved = jnp.dot(plan_low, gathered, preferred_element_type=jnp.float32)]
    slice x30 -> x0, local copies, waits for them, and re-layouts: 13.1 us -> none  [the longest x18 8.77 us: combined_all(): tail = jax.tree.map(lambda part: part[1:], pieces)]
  transfers between devices with their start and end apart: 8 -> 0, of which waited for: 7 -> 0; matrix products, arithmetic and copies ran while one was open for 1% -> 0% of each run, Pallas kernels for 0% -> 0%
where the time goes in v1:
time: 120 us
  Pallas kernels  116 us (97%)
  local copies, waits for them, and re-layouts  1.87 us (2%)
  between operations  1.81 us (2%)
    pallas_call x1, Pallas kernels, body(): pl.pallas_call(body_kernel, out_shape=(jax.ShapeDtypeStruct((rows, width)...  116 us

profile of v1, /device:TPU:1, one launch (start us, length us, event | category | flops | bytes accessed | tf_op | source)
XLA Modules:
  0.0 119.6 jit_solution(7180884274455607358)
XLA Ops:
  0.6 115.9 %sinkhorn.1 = (f32[512,256]{1,0:T(8,128)}, f32[1,128]{1,0:T(1,128)}) custom-call(bf16[512,1024]{1,0:T(8,128)(2,1)} %x_hbm.1, bf16[64,1024]{1,0:T(8,128)(2,1)} %y_hbm.1), custom_call_target="tpu_custom_call" | custom-call | tf_op jit(solution)/shard_map/sinkhorn/pallas_call | solution.py:540
  116.5 0.0 copy-start
  116.5 1.9 %copy.6 = f32[512,256]{1,0:T(8,128)} copy(f32[512,256]{1,0:T(8,128)} %get-tuple-element.8) | data formatting | bytes 1048576
  118.4 0.0 copy-done
Async XLA Ops:
  116.5 1.9 %copy-start = (f32[1,128]{1,0:T(1,128)S(1)}, f32[1,128]{1,0:T(1,128)}, u32[]{:S(2)}) copy-start(f32[1,128]{1,0:T(1,128)} %get-tuple-element.5) | copy-start | bytes 1540

commit v2 on v1

v2 whole, which is shorter than its diff:
```python
import math

import jax
import jax.numpy as jnp
from jax import lax
from jax.experimental import pallas as pl
from jax.experimental.pallas import tpu as pltpu
from jax.sharding import PartitionSpec as P

MESH = pl.DeviceIdType.MESH
EPSILON = 0.01
RATE = 2.0 * math.log2(math.e) / EPSILON
LIFT = 40.0

NX, NCORE, NY = 4, 2, 4
SUB = 32


def body_kernel(
    x_hbm, y_hbm, g_ref, loss_ref,
    xc, yg, aff, ex, plan_low, xn, top, tot, rowb, vcol, tcol,
    rs1, rr1, rs2, rr2,
    cxs1, cxr1, czs1, czr1, cxs2, cxr2, czs2, czr2,
    lzs, lzr, lxs, lxr, lys, lyr,
    term, half_in, part_out, part_in,
    local_sem, xcore_sem, gsend, ax_sem, az_sem, bz_sem, bx_sem,
    ex_send, ex_recv, hs_sem, hr_sem, ps_sem, pr_sem,
):
    rows, depth = x_hbm.shape
    shard = y_hbm.shape[0]
    nrow, ncol = aff.shape
    rate = RATE / depth
    nz = lax.axis_size("row") // (NX * NCORE)
    r = lax.axis_index("row")
    y = lax.axis_index("col")
    z = r // (NX * NCORE)
    x = (r // NCORE) % NX
    c = r % NCORE
    new_total = rows * lax.axis_size("row")
    old_total = shard * lax.axis_size("row") * lax.axis_size("col")
    lanes_a = 3 * depth // 8
    reach = nz // 2

    def dev(dz=0, dx=0, dc=0, dy=0):
        zz = lax.rem(z + dz + nz, nz)
        xx = lax.rem(x + dx + NX, NX)
        cc = lax.rem(c + dc, NCORE)
        yy = lax.rem(y + dy + NY, NY)
        return ((zz * NX + xx) * NCORE + cc, yy)

    z_peers = [dev(dz=d) for d in range(1, nz)]
    x_peers = [dev(dx=d) for d in range(1, NX)]
    y_peers = [dev(dy=d, dc=e) for d in range(NY) for e in range(NCORE) if d or e]

    barrier = pltpu.get_barrier_semaphore()
    everyone = z_peers + x_peers + y_peers
    for p in everyone:
        pl.semaphore_signal(barrier, inc=1, device_id=p, device_id_type=MESH)
    pl.semaphore_wait(barrier, len(everyone))

    part_lanes = {"a": pl.ds(0, lanes_a), "b": pl.ds(lanes_a, depth - lanes_a)}

    def region(dz, dx, part, half=None):
        slot = lax.rem(z + dz + nz, nz) * NX + lax.rem(x + dx + NX, NX)
        first = 0 if half is None else half * (shard // 2)
        count = shard if half is None else shard // 2
        start = pl.multiple_of(slot * shard + first, shard // 2)
        return yg.at[pl.ds(start, count), part_lanes[part]]

    def send(part, dst, sem, target, half=None, own=False):
        src = dst
        if own:
            src = y_hbm.at[:, part_lanes[part]]
        pltpu.make_async_remote_copy(
            src, dst, gsend.at[0 if part == "a" else 1], sem, device_id=target, device_id_type=MESH
        ).start()

    def arrived(ref, sem):
        pltpu.make_async_copy(ref, ref, sem).wait()

    zstep = (dev(dz=1), dev(dz=-1))
    zjump = (dev(dz=2), dev(dz=-2))
    xstep = (dev(dx=1), dev(dx=-1))
    xi_of = (0, -1, 1, 2)
    order_dz = [0] + [s * d for d in range(1, reach) for s in (-1, 1)] + [reach]
    place = {dz: i for i, dz in enumerate(order_dz)}

    def send_bx(dz, own=False):
        for way in (0, 1):
            send("b", region(dz, 0, "b"), bx_sem.at[place[dz], way], xstep[way], own=own)

    def send_az(xi, own=False):
        for way in (0, 1):
            send("a", region(0, xi_of[xi], "a"), az_sem.at[way, 0, xi], zstep[way], own=own)

    def on_ax(k):
        arrived(region(0, (-1, 1, 2)[k], "a"), ax_sem.at[k])
        send_az(1 + k)

    def on_az(way, d, xi):
        sign = -1 if way == 0 else 1
        here = region(sign * d, xi_of[xi], "a", None if d < reach else way)
        arrived(here, az_sem.at[way, d - 1, xi])
        if d < reach:
            half = None if d < reach - 1 else way
            send("a", region(sign * d, xi_of[xi], "a", half), az_sem.at[way, d, xi], zstep[way])

    def on_bz(way, d):
        sign = -1 if way == 0 else 1
        arrived(region(sign * d, 0, "b", None if d < reach else way), bz_sem.at[way, d - 1])
        if d == 2:
            send("b", region(sign * d, 0, "b"), bz_sem.at[way, 2], zstep[way])
            send("b", region(sign * d, 0, "b", way), bz_sem.at[way, 3], zjump[way])
        if d < reach:
            send_bx(sign * d)
        elif way == 1:
            send_bx(reach)

    def on_bx(dz, k):
        i = place[dz]
        if k < 2:
            dx = -1 if k == 0 else 1
            arrived(region(dz, dx, "b"), bx_sem.at[i, k])
            send("b", region(dz, dx, "b", k), bx_sem.at[i, 2 + k], xstep[k])
        else:
            arrived(region(dz, -2 if k == 2 else 2, "b", k - 2), bx_sem.at[i, k])

    own_slot = pl.ds(pl.multiple_of((z * NX + x) * shard, shard), shard)
    own_rows = pl.ds(pl.multiple_of(c * rows, rows), rows)
    other_rows = pl.ds(pl.multiple_of((1 - c) * rows, rows), rows)

    for way in (0, 1):
        send("b", region(0, 0, "b"), bz_sem.at[way, 0], zstep[way], own=True)
    for way in (0, 1):
        send("b", region(0, 0, "b"), bz_sem.at[way, 1], zjump[way], own=True)
    for k, target in enumerate((*xstep, dev(dx=2))):
        send("a", region(0, 0, "a"), ax_sem.at[k], target, own=True)
    send_az(0, own=True)
    send_bx(0, own=True)
    x_copy = pltpu.make_async_remote_copy(
        x_hbm, xc.at[own_rows], xcore_sem.at[0], xcore_sem.at[1], device_id=dev(dc=1), device_id_type=MESH
    )
    x_copy.start()
    x_local = pltpu.make_async_copy(x_hbm, xc.at[own_rows], local_sem.at[0])
    y_local = pltpu.make_async_copy(y_hbm, yg.at[own_slot], local_sem.at[1])
    x_local.start()
    y_local.start()

    top[...] = jnp.full(top.shape, -1e30, jnp.float32)
    tot[...] = jnp.zeros(tot.shape, jnp.float32)

    group = NX * shard
    tile = 256

    def compute(dz):
        col0 = pl.multiple_of(lax.rem(z + dz + nz, nz) * group, group)
        cols = pl.ds(col0, group)
        block = yg[cols, :]
        sq = jnp.square(block.astype(jnp.float32))
        part = sq[:, 0:128]
        for b in range(1, depth // 128):
            part = part + sq[:, b * 128 : (b + 1) * 128]
        half_norm = 0.5 * jnp.sum(jnp.transpose(part), axis=0, keepdims=True)
        inner = lax.dot_general(
            xc[...], block, (((1,), (1,)), ((), ())), preferred_element_type=jnp.float32
        )
        aff[:, cols] = inner - half_norm

        def step(i, carry):
            rs = pl.ds(pl.multiple_of(i * tile, tile), tile)
            best = top[rs, :]
            parts = [
                aff[rs, pl.ds(pl.multiple_of(col0 + b * 128, 128), 128)] for b in range(group // 128)
            ]
            high = best
            for val in parts:
                high = jnp.maximum(high, val)
            acc = tot[rs, :] * jnp.exp2((best - high) * rate)
            for val in parts:
                acc = acc + jnp.exp2((val - high) * rate)
            top[rs, :] = high
            tot[rs, :] = acc
            return carry

        lax.fori_loop(0, nrow // tile, step, 0)

    schedule = (
        (on_ax, 0), (on_ax, 1), (on_bz, 0, 1), (on_bz, 1, 1), (on_ax, 2), (on_bx, 0, 0), (on_bx, 0, 1),
        (on_bz, 0, 2), (on_bz, 1, 2), (on_az, 0, 1, 0), (on_az, 1, 1, 0), (on_bx, -1, 0), (on_bx, -1, 1),
        (on_az, 0, 1, 1), (on_az, 1, 1, 1), (on_az, 0, 1, 2), (on_az, 1, 1, 2), (on_bx, 1, 0), (on_bx, 1, 1),
        (on_az, 0, 1, 3), (on_az, 1, 1, 3), (on_bx, 0, 2), (on_bx, 0, 3), (compute, 0), (on_bz, 0, 3),
        (on_bz, 1, 3), (on_bx, -2, 0), (on_bx, -2, 1), (on_bz, 0, 4), (on_bz, 1, 4), (on_bx, 2, 0),
        (on_bx, 2, 1), (on_bx, -1, 2), (on_bx, -1, 3), (compute, -1), (on_az, 0, 2, 0), (on_az, 1, 2, 0),
        (on_bx, 1, 2), (on_bx, 1, 3), (on_az, 0, 2, 1), (on_az, 1, 2, 1), (compute, 1), (on_az, 0, 2, 2),
        (on_az, 1, 2, 2), (on_bx, -3, 0), (on_bx, -3, 1), (on_az, 0, 2, 3), (on_az, 1, 2, 3), (on_bx, 3, 0),
        (on_bx, 3, 1), (on_bx, -2, 2), (on_bx, -2, 3), (compute, -2), (on_az, 0, 3, 0), (on_az, 1, 3, 0),
        (on_az, 0, 3, 1), (on_az, 1, 3, 1), (on_bx, 4, 0), (on_bx, 4, 1), (on_az, 0, 3, 2), (on_az, 1, 3, 2),
        (on_bx, 2, 2), (on_bx, 2, 3), (compute, 2), (on_bx, -3, 2), (on_bx, -3, 3), (on_az, 0, 3, 3),
        (on_az, 1, 3, 3), (compute, -3), (on_bx, 3, 2), (on_bx, 3, 3), (on_az, 0, 4, 0), (on_az, 1, 4, 0),
        (compute, 3), (on_az, 0, 4, 1), (on_az, 1, 4, 1), (on_bx, 4, 2), (on_bx, 4, 3), (on_az, 0, 4, 2),
        (on_az, 1, 4, 2), (on_az, 0, 4, 3), (on_az, 1, 4, 3), (compute, 4),
    )
    stages = [[]]
    for act, *where in schedule:
        if act is compute:
            stages.append([])
        else:
            stages[-1].append((act, where))

    def stage(i, carry):
        for k, events in enumerate(stages[:nz]):

            @pl.when(i == k)
            def _(k=k, events=events):
                for act, where in events:
                    act(*where)
                if k == 0:
                    x_local.wait()
                    y_local.wait()
                    x_copy.wait()

        far = (i + 1) // 2
        compute(far - 2 * far * (i % 2))
        return carry

    lax.fori_loop(0, nz, stage, 0)

    def start(send_ref, recv_ref, i, peers):
        for j, p in enumerate(peers):
            pltpu.make_async_remote_copy(
                send_ref, recv_ref.at[j], ex_send.at[i], ex_recv.at[i], device_id=p, device_id_type=MESH
            ).start()

    def finish(recv_ref, i):
        pltpu.make_async_copy(recv_ref, recv_ref, ex_recv.at[i]).wait()
        pltpu.make_async_copy(recv_ref, recv_ref, ex_send.at[i]).wait()

    def to_rows(line):
        return jnp.transpose(jnp.broadcast_to(line, (128, nrow)))

    top_t = jnp.transpose(top[...])
    tot_t = jnp.transpose(tot[...])
    high = jnp.max(top_t, axis=0, keepdims=True)
    mass = jnp.sum(tot_t * jnp.exp2((top_t - high) * rate), axis=0, keepdims=True)
    rs1[:, 0:nrow] = high
    rs1[:, nrow : 2 * nrow] = mass
    start(rs1, rr1, 0, y_peers)

    def row_norms(i, carry):
        rs = pl.ds(pl.multiple_of(i * tile, tile), tile)
        part = jnp.zeros((tile, 128), jnp.float32)
        for b in range(depth // 128):
            part = part + jnp.square(xc[rs, b * 128 : (b + 1) * 128].astype(jnp.float32))
        xn[rs, :] = jnp.broadcast_to(0.5 * jnp.sum(part, axis=1, keepdims=True), (tile, 128))
        return carry

    lax.fori_loop(0, nrow // tile, row_norms, 0)
    finish(rr1, 0)
    highs = [high] + [rr1[j, :, 0:nrow] for j in range(len(y_peers))]
    masses = [mass] + [rr1[j, :, nrow : 2 * nrow] for j in range(len(y_peers))]
    high = highs[0]
    for v in highs[1:]:
        high = jnp.maximum(high, v)
    mass = sum(m * jnp.exp2((v - high) * rate) for v, m in zip(highs, masses))
    rowb[...] = to_rows(-high - (jnp.log2(mass) + math.log2(old_total)) / rate)

    nb = ncol // 128

    def fold(v, join):
        out = v[0:8]
        for i in range(1, v.shape[0] // 8):
            out = join(out, v[8 * i : 8 * i + 8])
        return out

    def highest(i, carry):
        rs = pl.ds(pl.multiple_of(i * SUB, SUB), SUB)
        rb = rowb[rs, :]
        out = []
        for b in range(nb):
            cs = pl.ds(b * 128, 128)
            a = rb + aff[rs, cs]
            ex[rs, cs] = a
            out.append(jnp.maximum(carry[b], fold(a, jnp.maximum)))
        return tuple(out)

    carry = lax.fori_loop(
        0, nrow // SUB, highest, tuple(jnp.full((8, 128), -3e38, jnp.float32) for _ in range(nb))
    )
    for b in range(nb):
        tcol[:, b * 128 : (b + 1) * 128] = jnp.max(carry[b], axis=0, keepdims=True) - LIFT / rate

    def scaled(i, carry):
        rs = pl.ds(pl.multiple_of(i * SUB, SUB), SUB)
        out = []
        for b in range(nb):
            cs = pl.ds(b * 128, 128)
            e = jnp.exp2((ex[rs, cs] - tcol[:, cs]) * rate)
            ex[rs, cs] = e
            out.append(carry[b] + fold(e, jnp.add))
        return tuple(out)

    zeros = tuple(jnp.zeros((8, 128), jnp.float32) for _ in range(nb))
    carry = lax.fori_loop(0, nrow // SUB, scaled, zeros)
    cxs1[:, 0:ncol] = tcol[...]
    for b in range(nb):
        cxs1[:, ncol + b * 128 : ncol + (b + 1) * 128] = jnp.sum(carry[b], axis=0, keepdims=True)

    def merge(own, recv, n):
        tops = [own[:, 0:ncol]] + [recv[j, :, 0:ncol] for j in range(n)]
        sums = [own[:, ncol:]] + [recv[j, :, ncol:] for j in range(n)]
        best = tops[0]
        for v in tops[1:]:
            best = jnp.maximum(best, v)
        return best, sum(s * jnp.exp2((v - best) * rate) for v, s in zip(tops, sums))

    start(cxs1, cxr1, 1, x_peers)
    finish(cxr1, 1)
    best, total = merge(cxs1[...], cxr1, len(x_peers))
    czs1[:, 0:ncol] = best
    czs1[:, ncol:] = total
    start(czs1, czr1, 2, z_peers)
    finish(czr1, 2)
    best, total = merge(czs1[...], czr1, len(z_peers))
    grow = 2.0 ** (2 * LIFT) / new_total
    vcol[...] = jnp.exp2((tcol[...] - best) * rate) * grow / total

    def again(sweep, carry):
        def row_sums(i, carry):
            rs = pl.ds(pl.multiple_of(i * SUB, SUB), SUB)
            acc = ex[rs, 0:128] * vcol[:, 0:128]
            for b in range(1, nb):
                cs = pl.ds(b * 128, 128)
                acc = acc + ex[rs, cs] * vcol[:, cs]
            tot[rs, :] = acc
            return carry

        lax.fori_loop(0, nrow // SUB, row_sums, 0)
        line = jnp.sum(jnp.transpose(tot[...]), axis=0, keepdims=True)
        i = 3 + 3 * sweep
        rs2[sweep] = line
        start(rs2.at[sweep], rr2.at[sweep], i, y_peers)
        finish(rr2.at[sweep], i)
        line = line + sum(rr2[sweep, j] for j in range(len(y_peers)))
        rowb[...] = to_rows((2.0 ** (2 * LIFT) / old_total) / line)

        def col_sums(i, carry):
            rs = pl.ds(pl.multiple_of(i * SUB, SUB), SUB)
            rb = rowb[rs, :]
            return tuple(
                carry[b] + fold(ex[rs, pl.ds(b * 128, 128)] * rb, jnp.add) for b in range(nb)
            )

        sums = lax.fori_loop(0, nrow // SUB, col_sums, zeros)
        for b in range(nb):
            cs = pl.ds(b * 128, 128)
            cxs2[sweep, :, cs] = vcol[:, cs] * jnp.sum(sums[b], axis=0, keepdims=True)
        start(cxs2.at[sweep], cxr2.at[sweep], i + 1, x_peers)
        finish(cxr2.at[sweep], i + 1)
        czs2[sweep] = cxs2[sweep] + sum(cxr2[sweep, j] for j in range(len(x_peers)))
        start(czs2.at[sweep], czr2.at[sweep], i + 2, z_peers)
        finish(czr2.at[sweep], i + 2)
        total = czs2[sweep] + sum(czr2[sweep, j] for j in range(len(z_peers)))
        vcol[...] = vcol[...] * (grow / total)
        return carry

    lax.fori_loop(0, 2, again, 0)

    def planned(i, carry):
        rs = pl.ds(pl.multiple_of(i * SUB, SUB), SUB)
        rb = rowb[rs, :] * 2.0 ** (-2 * LIFT)
        xs = xn[rs, :]
        mass = jnp.zeros((SUB, 128), jnp.float32)
        part = jnp.zeros((SUB, 128), jnp.float32)
        for b in range(nb):
            cs = pl.ds(b * 128, 128)
            p = ex[rs, cs] * rb * vcol[:, cs]
            plan_low[rs, cs] = p.astype(jnp.bfloat16)
            mass = mass + p
            part = part + p * (xs - aff[rs, cs])
        tot[rs, :] = mass
        return carry + fold(part, jnp.add)

    part = lax.fori_loop(0, nrow // SUB, planned, jnp.zeros((8, 128), jnp.float32))
    lys[...] = jnp.sum(part, axis=0, keepdims=True)
    start(lys, lyr, 11, y_peers)

    def row_mass(i, carry):
        rs = pl.ds(pl.multiple_of(i * tile, tile), tile)
        tot[rs, :] = jnp.broadcast_to(jnp.sum(tot[rs, :], axis=1, keepdims=True), (tile, 128))
        return carry

    lax.fori_loop(0, nrow // tile, row_mass, 0)

    width = g_ref.shape[1]
    def turn(ci):
        return jnp.where(ci == 0, 2, jnp.where(ci == 1, 1, jnp.where(ci == 2, 3, 0)))

    def product(ci):
        q = lax.rem(y + turn(ci), NY)
        lanes = pl.ds(pl.multiple_of(q * width, width), width)
        moved = jnp.dot(plan_low[...], yg[:, lanes], preferred_element_type=jnp.float32)
        m = tot[...]
        for b in range(width // 128):
            cs = pl.ds(pl.multiple_of(q * width + b * 128, 128), 128)
            term[ci, :, b * 128 : (b + 1) * 128] = (
                xc[:, cs].astype(jnp.float32) * m - moved[:, b * 128 : (b + 1) * 128]
            )
        half_copy(ci).start()

    def half_copy(ci):
        return pltpu.make_async_remote_copy(
            term.at[ci, other_rows], half_in.at[ci], hs_sem.at[ci], hr_sem.at[ci],
            device_id=dev(dc=1), device_id_type=MESH,
        )

    def part_copy(ci):
        return pltpu.make_async_remote_copy(
            part_out.at[ci], part_in.at[ci], ps_sem.at[ci], pr_sem.at[ci],
            device_id=dev(dy=turn(ci)), device_id_type=MESH,
        )

    def pass_on(ci):
        half_copy(ci).wait()
        part_out[ci] = (term[ci, own_rows, :] + half_in[ci]).astype(jnp.bfloat16)
        part_copy(ci).start()

    def chunk(ci, carry):
        product(ci)

        @pl.when(ci > 0)
        def _():
            pass_on(ci - 1)

        @pl.when(ci == 2)
        def _():
            finish(lyr, 11)
            lzs[...] = lys[...] + sum(lyr[j] for j in range(len(y_peers)))
            start(lzs, lzr, 9, z_peers)

        return carry

    lax.fori_loop(0, NY, chunk, 0)
    half_copy(3).wait()
    term[3, own_rows, :] = term[3, own_rows, :] + half_in[3]
    finish(lzr, 9)
    lxs[...] = lzs[...] + sum(lzr[j] for j in range(len(z_peers)))
    start(lxs, lxr, 10, x_peers)
    part_copy(0).wait()
    part_copy(1).wait()
    term[3, own_rows, :] = (
        term[3, own_rows, :] + part_in[0].astype(jnp.float32) + part_in[1].astype(jnp.float32)
    )
    finish(lxr, 10)
    loss = lxs[...] + sum(lxr[j] for j in range(len(x_peers)))
    loss_ref[...] = jnp.broadcast_to(jnp.sum(loss, axis=1, keepdims=True) * (2.0 / depth), loss_ref.shape)
    part_copy(2).wait()
    g_ref[...] = float(new_total) * (term[3, own_rows, :] + part_in[2].astype(jnp.float32))
    others = (nz * NX - 1) * shard
    for i, part in ((0, "a"), (1, "b")):
        sent = yg.at[pl.ds(0, others), part_lanes[part]]
        pltpu.make_async_copy(sent, sent, gsend.at[i]).wait()


def solution(mesh):
    def body(new_embeddings, old_vectors):
        rows, depth = new_embeddings.shape
        shard = old_vectors.shape[0]
        nz = lax.axis_size("row") // (NX * NCORE)
        nrow, ncol = rows * NCORE, shard * nz * NX
        width = depth // NY
        f32, bf16 = jnp.float32, jnp.bfloat16
        ny, npx, npz = NY * NCORE - 1, NX - 1, nz - 1
        dma = pltpu.SemaphoreType.DMA
        scratch = [
            pltpu.VMEM((nrow, depth), bf16),
            pltpu.VMEM((ncol, depth), bf16),
            pltpu.VMEM((nrow, ncol), f32),
            pltpu.VMEM((nrow, ncol), f32),
            pltpu.VMEM((nrow, ncol), bf16),
            pltpu.VMEM((nrow, 128), f32),
            pltpu.VMEM((nrow, 128), f32),
            pltpu.VMEM((nrow, 128), f32),
            pltpu.VMEM((nrow, 128), f32),
            pltpu.VMEM((1, ncol), f32),
            pltpu.VMEM((1, ncol), f32),
            pltpu.VMEM((1, 2 * nrow), f32),
            pltpu.VMEM((ny, 1, 2 * nrow), f32),
            pltpu.VMEM((2, 1, nrow), f32),
            pltpu.VMEM((2, ny, 1, nrow), f32),
            pltpu.VMEM((1, 2 * ncol), f32),
            pltpu.VMEM((npx, 1, 2 * ncol), f32),
            pltpu.VMEM((1, 2 * ncol), f32),
            pltpu.VMEM((npz, 1, 2 * ncol), f32),
            pltpu.VMEM((2, 1, ncol), f32),
            pltpu.VMEM((2, npx, 1, ncol), f32),
            pltpu.VMEM((2, 1, ncol), f32),
            pltpu.VMEM((2, npz, 1, ncol), f32),
            pltpu.VMEM((1, 128), f32),
            pltpu.VMEM((npz, 1, 128), f32),
            pltpu.VMEM((1, 128), f32),
            pltpu.VMEM((npx, 1, 128), f32),
            pltpu.VMEM((1, 128), f32),
            pltpu.VMEM((ny, 1, 128), f32),
            pltpu.VMEM((4, nrow, width), f32),
            pltpu.VMEM((4, rows, width), f32),
            pltpu.VMEM((3, rows, width), bf16),
            pltpu.VMEM((3, rows, width), bf16),
            dma((2,)),
            dma((2,)),
            dma((2,)),
            dma((3,)),
            dma((2, nz // 2, 4)),
            dma((2, nz // 2)),
            dma((nz, 4)),
            dma((12,)),
            dma((12,)),
            dma((4,)),
            dma((4,)),
            dma((3,)),
            dma((3,)),
        ]
        gradient, loss = pl.pallas_call(
            body_kernel,
            out_shape=(
                pltpu.VMEM((rows, width), f32),
                pltpu.VMEM((1, 128), f32),
            ),
            in_specs=[pl.BlockSpec(memory_space=pl.ANY)] * 2,
            out_specs=[pl.BlockSpec(memory_space=pltpu.VMEM)] * 2,
            scratch_shapes=scratch,
            compiler_params=pltpu.CompilerParams(
                collective_id=0, has_side_effects=True, vmem_limit_bytes=56 << 20
            ),
            name="sinkhorn",
        )(new_embeddings, old_vectors)
        return gradient, loss[0, 0]

    placed = (P("row", None), P(("col", "row"), None))
    return jax.shard_map(
        body, mesh=mesh, in_specs=placed, out_specs=(P("row", "col"), P()), check_vma=False
    )
```

time: 120 us -> 109 us (0.908)
  Pallas kernels: 116 us -> 106 us
    pallas_call x1, Pallas kernels: 116 us -> 106 us  [body(): pl.pallas_call(body_kernel, out_shape=(pltpu.VMEM((rows, width), f32), pl...]
where the time goes in v2:
time: 109 us; the launch traced here: 108 us
  Pallas kernels  106 us (97%)
  between operations  1.8 us (2%)
    pallas_call x1, Pallas kernels, body(): pl.pallas_call(body_kernel, out_shape=(pltpu.VMEM((rows, width), f32), pl...  106 us

profile of v2, /device:TPU:1, one launch (start us, length us, event | category | flops | bytes accessed | tf_op | source)
XLA Modules:
  0.0 108.5 jit_solution(3103592664711054641)
XLA Ops:
  0.6 105.9 %sinkhorn.1 = (f32[512,256]{1,0:T(8,128)S(1)}, f32[1,128]{1,0:T(1,128)S(1)}) custom-call(bf16[512,1024]{1,0:T(8,128)(2,1)} %x_hbm.1, bf16[64,1024]{1,0:T(8,128)(2,1)} %y_hbm.1), custom_call_target="tpu_custom_call" | custom-call | tf_op jit(solution)/shard_map/sinkhorn/pallas_call | solution.py:522
  106.5 0.8 copy.6

commit v3 on v2

--- a/solution.py
+++ b/solution.py
@@ -13,12 +13,12 @@
 LIFT = 40.0
 
 NX, NCORE, NY = 4, 2, 4
-SUB = 32
+SUB = 64
 
 
 def body_kernel(
     x_hbm, y_hbm, g_ref, loss_ref,
-    xc, yg, aff, ex, plan_low, xn, top, tot, rowb, vcol, tcol,
+    xc, yg, aff, ex, plan_low, xn, top, tot, rowb, vcol, tcol, loss_part,
     rs1, rr1, rs2, rr2,
     cxs1, cxr1, czs1, czr1, cxs2, cxr2, czs2, czr2,
     lzs, lzr, lxs, lxr, lys, lyr,
@@ -187,18 +187,18 @@
     schedule = (
         (on_ax, 0), (on_ax, 1), (on_bz, 0, 1), (on_bz, 1, 1), (on_ax, 2), (on_bx, 0, 0), (on_bx, 0, 1),
         (on_bz, 0, 2), (on_bz, 1, 2), (on_az, 0, 1, 0), (on_az, 1, 1, 0), (on_bx, -1, 0), (on_bx, -1, 1),
-        (on_az, 0, 1, 1), (on_az, 1, 1, 1), (on_az, 0, 1, 2), (on_az, 1, 1, 2), (on_bx, 1, 0), (on_bx, 1, 1),
-        (on_az, 0, 1, 3), (on_az, 1, 1, 3), (on_bx, 0, 2), (on_bx, 0, 3), (compute, 0), (on_bz, 0, 3),
-        (on_bz, 1, 3), (on_bx, -2, 0), (on_bx, -2, 1), (on_bz, 0, 4), (on_bz, 1, 4), (on_bx, 2, 0),
-        (on_bx, 2, 1), (on_bx, -1, 2), (on_bx, -1, 3), (compute, -1), (on_az, 0, 2, 0), (on_az, 1, 2, 0),
-        (on_bx, 1, 2), (on_bx, 1, 3), (on_az, 0, 2, 1), (on_az, 1, 2, 1), (compute, 1), (on_az, 0, 2, 2),
-        (on_az, 1, 2, 2), (on_bx, -3, 0), (on_bx, -3, 1), (on_az, 0, 2, 3), (on_az, 1, 2, 3), (on_bx, 3, 0),
-        (on_bx, 3, 1), (on_bx, -2, 2), (on_bx, -2, 3), (compute, -2), (on_az, 0, 3, 0), (on_az, 1, 3, 0),
-        (on_az, 0, 3, 1), (on_az, 1, 3, 1), (on_bx, 4, 0), (on_bx, 4, 1), (on_az, 0, 3, 2), (on_az, 1, 3, 2),
-        (on_bx, 2, 2), (on_bx, 2, 3), (compute, 2), (on_bx, -3, 2), (on_bx, -3, 3), (on_az, 0, 3, 3),
-        (on_az, 1, 3, 3), (compute, -3), (on_bx, 3, 2), (on_bx, 3, 3), (on_az, 0, 4, 0), (on_az, 1, 4, 0),
-        (compute, 3), (on_az, 0, 4, 1), (on_az, 1, 4, 1), (on_bx, 4, 2), (on_bx, 4, 3), (on_az, 0, 4, 2),
-        (on_az, 1, 4, 2), (on_az, 0, 4, 3), (on_az, 1, 4, 3), (compute, 4),
+        (on_az, 0, 1, 1), (on_az, 1, 1, 1), (on_bx, 1, 0), (on_bx, 1, 1), (on_az, 0, 1, 2), (on_az, 1, 1, 2),
+        (on_bx, 0, 2), (on_bx, 0, 3), (compute, 0), (on_az, 0, 1, 3), (on_az, 1, 1, 3), (on_bx, -2, 0),
+        (on_bx, -2, 1), (on_bz, 0, 3), (on_bz, 1, 3), (on_bx, 2, 0), (on_bx, 2, 1), (on_bz, 0, 4),
+        (on_bz, 1, 4), (on_bx, -1, 2), (on_bx, -1, 3), (compute, -1), (on_az, 0, 2, 0), (on_az, 1, 2, 0),
+        (on_bx, 1, 2), (on_bx, 1, 3), (compute, 1), (on_az, 0, 2, 1), (on_az, 1, 2, 1), (on_az, 0, 2, 2),
+        (on_az, 1, 2, 2), (on_bx, -3, 0), (on_bx, -3, 1), (on_az, 0, 2, 3), (on_az, 1, 2, 3), (on_bx, -2, 2),
+        (on_bx, -2, 3), (compute, -2), (on_az, 0, 3, 0), (on_bx, 3, 0), (on_az, 1, 3, 0), (on_bx, 3, 1),
+        (on_bx, 2, 2), (on_bx, 2, 3), (compute, 2), (on_az, 0, 3, 1), (on_az, 1, 3, 1), (on_az, 0, 3, 2),
+        (on_az, 1, 3, 2), (on_bx, 4, 0), (on_bx, 4, 1), (on_az, 0, 3, 3), (on_az, 1, 3, 3), (on_bx, -3, 2),
+        (on_bx, -3, 3), (compute, -3), (on_bx, 3, 2), (on_bx, 3, 3), (compute, 3), (on_az, 0, 4, 0),
+        (on_az, 1, 4, 0), (on_az, 0, 4, 1), (on_az, 1, 4, 1), (on_az, 0, 4, 2), (on_az, 1, 4, 2),
+        (on_bx, 4, 2), (on_bx, 4, 3), (on_az, 0, 4, 3), (on_az, 1, 4, 3), (compute, 4),
     )
     stages = [[]]
     for act, *where in schedule:
@@ -289,100 +289,138 @@
     for b in range(nb):
         tcol[:, b * 128 : (b + 1) * 128] = jnp.max(carry[b], axis=0, keepdims=True) - LIFT / rate
 
-    def scaled(i, carry):
-        rs = pl.ds(pl.multiple_of(i * SUB, SUB), SUB)
-        out = []
-        for b in range(nb):
-            cs = pl.ds(b * 128, 128)
-            e = jnp.exp2((ex[rs, cs] - tcol[:, cs]) * rate)
-            ex[rs, cs] = e
-            out.append(carry[b] + fold(e, jnp.add))
-        return tuple(out)
-
-    zeros = tuple(jnp.zeros((8, 128), jnp.float32) for _ in range(nb))
-    carry = lax.fori_loop(0, nrow // SUB, scaled, zeros)
-    cxs1[:, 0:ncol] = tcol[...]
-    for b in range(nb):
-        cxs1[:, ncol + b * 128 : ncol + (b + 1) * 128] = jnp.sum(carry[b], axis=0, keepdims=True)
-
-    def merge(own, recv, n):
-        tops = [own[:, 0:ncol]] + [recv[j, :, 0:ncol] for j in range(n)]
-        sums = [own[:, ncol:]] + [recv[j, :, ncol:] for j in range(n)]
+    hb = nb // 2
+    hc = ncol // 2
+    spans = [range(h * hb, (h + 1) * hb) for h in range(2)]
+    sides = [pl.ds(h * hc, hc) for h in range(2)]
+    zeros = tuple(jnp.zeros((8, 128), jnp.float32) for _ in range(hb))
+
+    def column_exchange(xs, xr, zs, zr, i, produce, merge, use):
+        for h in range(2):
+            produce(h)
+            start(xs.at[h], xr.at[h], i + h, x_peers)
+        for h in range(2):
+            finish(xr.at[h], i + h)
+            zs[h] = merge(xs, xr, h, len(x_peers))
+            start(zs.at[h], zr.at[h], i + 2 + h, z_peers)
+        for h in range(2):
+            finish(zr.at[h], i + 2 + h)
+            use(h, merge(zs, zr, h, len(z_peers)))
+
+    def row_sums(h):
+        def step(i, carry):
+            rs = pl.ds(pl.multiple_of(i * SUB, SUB), SUB)
+            acc = tot[rs, :] if h else None
+            for b in spans[h]:
+                cs = pl.ds(b * 128, 128)
+                v = ex[rs, cs] * vcol[:, cs]
+                acc = v if acc is None else acc + v
+            tot[rs, :] = acc
+            return carry
+
+        lax.fori_loop(0, nrow // SUB, step, 0)
+
+    grow = 2.0 ** (2 * LIFT) / new_total
+
+    def scaled(h):
+        def step(i, carry):
+            rs = pl.ds(pl.multiple_of(i * SUB, SUB), SUB)
+            out = []
+            for n, b in enumerate(spans[h]):
+                cs = pl.ds(b * 128, 128)
+                e = jnp.exp2((ex[rs, cs] - tcol[:, cs]) * rate)
+                ex[rs, cs] = e
+                out.append(carry[n] + fold(e, jnp.add))
+            return tuple(out)
+
+        sums = lax.fori_loop(0, nrow // SUB, step, zeros)
+        cxs1[h, :, 0:hc] = tcol[:, sides[h]]
+        for n in range(hb):
+            cxs1[h, :, hc + n * 128 : hc + (n + 1) * 128] = jnp.sum(sums[n], axis=0, keepdims=True)
+
+    def merge_shifted(own, recv, h, n):
+        tops = [own[h, :, 0:hc]] + [recv[h, j, :, 0:hc] for j in range(n)]
+        sums = [own[h, :, hc:]] + [recv[h, j, :, hc:] for j in range(n)]
         best = tops[0]
         for v in tops[1:]:
             best = jnp.maximum(best, v)
-        return best, sum(s * jnp.exp2((v - best) * rate) for v, s in zip(tops, sums))
-
-    start(cxs1, cxr1, 1, x_peers)
-    finish(cxr1, 1)
-    best, total = merge(cxs1[...], cxr1, len(x_peers))
-    czs1[:, 0:ncol] = best
-    czs1[:, ncol:] = total
-    start(czs1, czr1, 2, z_peers)
-    finish(czr1, 2)
-    best, total = merge(czs1[...], czr1, len(z_peers))
-    grow = 2.0 ** (2 * LIFT) / new_total
-    vcol[...] = jnp.exp2((tcol[...] - best) * rate) * grow / total
+        total = sum(t * jnp.exp2((v - best) * rate) for v, t in zip(tops, sums))
+        return jnp.concatenate([best, total], axis=1)
+
+    def first_factor(h, both):
+        vcol[:, sides[h]] = jnp.exp2((tcol[:, sides[h]] - both[:, 0:hc]) * rate) * grow / both[:, hc:]
+        row_sums(h)
+
+    column_exchange(cxs1, cxr1, czs1, czr1, 1, scaled, merge_shifted, first_factor)
+
+    loss_part[...] = jnp.zeros((8, 128), jnp.float32)
+
+    def planned(h):
+        def step(i, carry):
+            rs = pl.ds(pl.multiple_of(i * SUB, SUB), SUB)
+            rb = rowb[rs, :] * 2.0 ** (-2 * LIFT)
+            xs = xn[rs, :]
+            mass = tot[rs, :] if h else jnp.zeros((SUB, 128), jnp.float32)
+            part = jnp.zeros((SUB, 128), jnp.float32)
+            for b in spans[h]:
+                cs = pl.ds(b * 128, 128)
+                p = ex[rs, cs] * rb * vcol[:, cs]
+                plan_low[rs, cs] = p.astype(jnp.bfloat16)
+                mass = mass + p
+                part = part + p * (xs - aff[rs, cs])
+            tot[rs, :] = mass
+            return carry + fold(part, jnp.add)
+
+        loss_part[...] = lax.fori_loop(0, nrow // SUB, step, loss_part[...])
+
+    def merge_sums(own, recv, h, n):
+        return own[h] + sum(recv[h, j] for j in range(n))
 
     def again(sweep, carry):
-        def row_sums(i, carry):
-            rs = pl.ds(pl.multiple_of(i * SUB, SUB), SUB)
-            acc = ex[rs, 0:128] * vcol[:, 0:128]
-            for b in range(1, nb):
-                cs = pl.ds(b * 128, 128)
-                acc = acc + ex[rs, cs] * vcol[:, cs]
-            tot[rs, :] = acc
-            return carry
-
-        lax.fori_loop(0, nrow // SUB, row_sums, 0)
         line = jnp.sum(jnp.transpose(tot[...]), axis=0, keepdims=True)
-        i = 3 + 3 * sweep
+        i = 5 + 5 * sweep
         rs2[sweep] = line
         start(rs2.at[sweep], rr2.at[sweep], i, y_peers)
         finish(rr2.at[sweep], i)
         line = line + sum(rr2[sweep, j] for j in range(len(y_peers)))
         rowb[...] = to_rows((2.0 ** (2 * LIFT) / old_total) / line)
 
-        def col_sums(i, carry):
-            rs = pl.ds(pl.multiple_of(i * SUB, SUB), SUB)
-            rb = rowb[rs, :]
-            return tuple(
-                carry[b] + fold(ex[rs, pl.ds(b * 128, 128)] * rb, jnp.add) for b in range(nb)
-            )
-
-        sums = lax.fori_loop(0, nrow // SUB, col_sums, zeros)
-        for b in range(nb):
-            cs = pl.ds(b * 128, 128)
-            cxs2[sweep, :, cs] = vcol[:, cs] * jnp.sum(sums[b], axis=0, keepdims=True)
-        start(cxs2.at[sweep], cxr2.at[sweep], i + 1, x_peers)
-        finish(cxr2.at[sweep], i + 1)
-        czs2[sweep] = cxs2[sweep] + sum(cxr2[sweep, j] for j in range(len(x_peers)))
-        start(czs2.at[sweep], czr2.at[sweep], i + 2, z_peers)
-        finish(czr2.at[sweep], i + 2)
-        total = czs2[sweep] + sum(czr2[sweep, j] for j in range(len(z_peers)))
-        vcol[...] = vcol[...] * (grow / total)
+        def col_sums(h):
+            def step(k, sums):
+                rs = pl.ds(pl.multiple_of(k * SUB, SUB), SUB)
+                rb = rowb[rs, :]
+                return tuple(
+                    sums[n] + fold(ex[rs, pl.ds(b * 128, 128)] * rb, jnp.add)
+                    for n, b in enumerate(spans[h])
+                )
+
+            sums = lax.fori_loop(0, nrow // SUB, step, zeros)
+            for n, b in enumerate(spans[h]):
+                cxs2[sweep, h, :, n * 128 : (n + 1) * 128] = vcol[:, b * 128 : (b + 1) * 128] * jnp.sum(
+                    sums[n], axis=0, keepdims=True
+                )
+
+        def next_factor(h, total):
+            vcol[:, sides[h]] = vcol[:, sides[h]] * (grow / total)
+
+            @pl.when(sweep == 0)
+            def _():
+                row_sums(h)
+
+            @pl.when(sweep == 1)
+            def _():
+                planned(h)
+
+        column_exchange(
+            cxs2.at[sweep], cxr2.at[sweep], czs2.at[sweep], czr2.at[sweep], i + 1,
+            col_sums, merge_sums, next_factor,
+        )
         return carry
 
     lax.fori_loop(0, 2, again, 0)
 
-    def planned(i, carry):
-        rs = pl.ds(pl.multiple_of(i * SUB, SUB), SUB)
-        rb = rowb[rs, :] * 2.0 ** (-2 * LIFT)
-        xs = xn[rs, :]
-        mass = jnp.zeros((SUB, 128), jnp.float32)
-        part = jnp.zeros((SUB, 128), jnp.float32)
-        for b in range(nb):
-            cs = pl.ds(b * 128, 128)
-            p = ex[rs, cs] * rb * vcol[:, cs]
-            plan_low[rs, cs] = p.astype(jnp.bfloat16)
-            mass = mass + p
-            part = part + p * (xs - aff[rs, cs])
-        tot[rs, :] = mass
-        return carry + fold(part, jnp.add)
-
-    part = lax.fori_loop(0, nrow // SUB, planned, jnp.zeros((8, 128), jnp.float32))
-    lys[...] = jnp.sum(part, axis=0, keepdims=True)
-    start(lys, lyr, 11, y_peers)
+    lys[...] = jnp.sum(loss_part[...], axis=0, keepdims=True)
+    start(lys, lyr, 15, y_peers)
 
     def row_mass(i, carry):
         rs = pl.ds(pl.multiple_of(i * tile, tile), tile)
@@ -433,24 +471,24 @@
 
         @pl.when(ci == 2)
         def _():
-            finish(lyr, 11)
+            finish(lyr, 15)
             lzs[...] = lys[...] + sum(lyr[j] for j in range(len(y_peers)))
-            start(lzs, lzr, 9, z_peers)
+            start(lzs, lzr, 16, z_peers)
 
         return carry
 
     lax.fori_loop(0, NY, chunk, 0)
     half_copy(3).wait()
     term[3, own_rows, :] = term[3, own_rows, :] + half_in[3]
-    finish(lzr, 9)
+    finish(lzr, 16)
     lxs[...] = lzs[...] + sum(lzr[j] for j in range(len(z_peers)))
-    start(lxs, lxr, 10, x_peers)
+    start(lxs, lxr, 17, x_peers)
     part_copy(0).wait()
     part_copy(1).wait()
     term[3, own_rows, :] = (
         term[3, own_rows, :] + part_in[0].astype(jnp.float32) + part_in[1].astype(jnp.float32)
     )
-    finish(lxr, 10)
+    finish(lxr, 17)
     loss = lxs[...] + sum(lxr[j] for j in range(len(x_peers)))
     loss_ref[...] = jnp.broadcast_to(jnp.sum(loss, axis=1, keepdims=True) * (2.0 / depth), loss_ref.shape)
     part_copy(2).wait()
@@ -483,18 +521,19 @@
             pltpu.VMEM((nrow, 128), f32),
             pltpu.VMEM((1, ncol), f32),
             pltpu.VMEM((1, ncol), f32),
+            pltpu.VMEM((8, 128), f32),
             pltpu.VMEM((1, 2 * nrow), f32),
             pltpu.VMEM((ny, 1, 2 * nrow), f32),
             pltpu.VMEM((2, 1, nrow), f32),
             pltpu.VMEM((2, ny, 1, nrow), f32),
-            pltpu.VMEM((1, 2 * ncol), f32),
-            pltpu.VMEM((npx, 1, 2 * ncol), f32),
-            pltpu.VMEM((1, 2 * ncol), f32),
-            pltpu.VMEM((npz, 1, 2 * ncol), f32),
             pltpu.VMEM((2, 1, ncol), f32),
             pltpu.VMEM((2, npx, 1, ncol), f32),
             pltpu.VMEM((2, 1, ncol), f32),
             pltpu.VMEM((2, npz, 1, ncol), f32),
+            pltpu.VMEM((2, 2, 1, ncol // 2), f32),
+            pltpu.VMEM((2, 2, npx, 1, ncol // 2), f32),
+            pltpu.VMEM((2, 2, 1, ncol // 2), f32),
+            pltpu.VMEM((2, 2, npz, 1, ncol // 2), f32),
             pltpu.VMEM((1, 128), f32),
             pltpu.VMEM((npz, 1, 128), f32),
             pltpu.VMEM((1, 128), f32),
@@ -512,8 +551,8 @@
             dma((2, nz // 2, 4)),
             dma((2, nz // 2)),
             dma((nz, 4)),
-            dma((12,)),
-            dma((12,)),
+            dma((18,)),
+            dma((18,)),
             dma((4,)),
             dma((4,)),
             dma((3,)),

time: 109 us -> 105 us (0.963)
  Pallas kernels: 106 us -> 102 us
    pallas_call x1, Pallas kernels: 106 us -> 102 us  [body(): pl.pallas_call(body_kernel, out_shape=(pltpu.VMEM((rows, width), f32), pl...]
where the time goes in v3:
time: 105 us
  Pallas kernels  102 us (97%)
  between operations  1.8 us (2%)
    pallas_call x1, Pallas kernels, body(): pl.pallas_call(body_kernel, out_shape=(pltpu.VMEM((rows, width), f32), pl...  102 us

profile of v3, /device:TPU:1, one launch (start us, length us, event | category | flops | bytes accessed | tf_op | source)
XLA Modules:
  0.0 104.8 jit_solution(990312949093298625)
XLA Ops:
  0.6 102.2 %sinkhorn.1 = (f32[512,256]{1,0:T(8,128)S(1)}, f32[1,128]{1,0:T(1,128)S(1)}) custom-call(bf16[512,1024]{1,0:T(8,128)(2,1)} %x_hbm.1, bf16[64,1024]{1,0:T(8,128)(2,1)} %y_hbm.1), custom_call_target="tpu_custom_call" | custom-call | tf_op jit(solution)/shard_map/sinkhorn/pallas_call | solution.py:561
  102.8 0.8 copy.6

commit v4 on v3

--- a/solution.py
+++ b/solution.py
@@ -131,12 +131,12 @@
 
     for way in (0, 1):
         send("b", region(0, 0, "b"), bz_sem.at[way, 0], zstep[way], own=True)
+    for k, target in enumerate((*xstep, dev(dx=2))):
+        send("a", region(0, 0, "a"), ax_sem.at[k], target, own=True)
     for way in (0, 1):
         send("b", region(0, 0, "b"), bz_sem.at[way, 1], zjump[way], own=True)
-    for k, target in enumerate((*xstep, dev(dx=2))):
-        send("a", region(0, 0, "a"), ax_sem.at[k], target, own=True)
+    send_bx(0, own=True)
     send_az(0, own=True)
-    send_bx(0, own=True)
     x_copy = pltpu.make_async_remote_copy(
         x_hbm, xc.at[own_rows], xcore_sem.at[0], xcore_sem.at[1], device_id=dev(dc=1), device_id_type=MESH
     )

time: 105 us -> 105 us (level)
  no operation moved by 1% of the time
where the time goes in v4:
time: 105 us
  Pallas kernels  102 us (97%)
  between operations  1.8 us (2%)
    pallas_call x1, Pallas kernels, body(): pl.pallas_call(body_kernel, out_shape=(pltpu.VMEM((rows, width), f32), pl...  102 us

profile of v4, /device:TPU:1, one launch (start us, length us, event | category | flops | bytes accessed | tf_op | source)
XLA Modules:
  0.0 104.8 jit_solution(4652680178126201871)
XLA Ops:
  0.6 102.2 %sinkhorn.1 = (f32[512,256]{1,0:T(8,128)S(1)}, f32[1,128]{1,0:T(1,128)S(1)}) custom-call(bf16[512,1024]{1,0:T(8,128)(2,1)} %x_hbm.1, bf16[64,1024]{1,0:T(8,128)(2,1)} %y_hbm.1), custom_call_target="tpu_custom_call" | custom-call | tf_op jit(solution)/shard_map/sinkhorn/pallas_call | solution.py:561
  102.8 0.8 copy.6

commit v5 on v4

--- a/solution.py
+++ b/solution.py
@@ -431,7 +431,7 @@
 
     width = g_ref.shape[1]
     def turn(ci):
-        return jnp.where(ci == 0, 2, jnp.where(ci == 1, 1, jnp.where(ci == 2, 3, 0)))
+        return jnp.where(ci == 0, 1, jnp.where(ci == 1, 3, jnp.where(ci == 2, 2, 0)))
 
     def product(ci):
         q = lax.rem(y + turn(ci), NY)

time: 105 us -> 104 us (level)
  no operation moved by 1% of the time
where the time goes in v5:
time: 104 us
  Pallas kernels  102 us (98%)
  between operations  1.8 us (2%)
    pallas_call x1, Pallas kernels, body(): pl.pallas_call(body_kernel, out_shape=(pltpu.VMEM((rows, width), f32), pl...  102 us

profile of v5, /device:TPU:1, one launch (start us, length us, event | category | flops | bytes accessed | tf_op | source)
XLA Modules:
  0.0 104.4 jit_solution(10436850710423525402)
XLA Ops:
  0.6 101.8 %sinkhorn.1 = (f32[512,256]{1,0:T(8,128)S(1)}, f32[1,128]{1,0:T(1,128)S(1)}) custom-call(bf16[512,1024]{1,0:T(8,128)(2,1)} %x_hbm.1, bf16[64,1024]{1,0:T(8,128)(2,1)} %y_hbm.1), custom_call_target="tpu_custom_call" | custom-call | tf_op jit(solution)/shard_map/sinkhorn/pallas_call | solution.py:561
  102.4 0.8 copy.6
